TPU v7x, 128 devices: a whole 4x4x4 slice. The times are simulated.
128 devices in a mesh: grp: 4 (over x), mem: 32 (over z, y, core).
Axes of the slice: x: 4, y: 4, z: 4, core: 2. Of those that a mesh axis runs over, the one named last changes fastest.
Arguments:
- user_rows: bfloat16 [16384, 2048], P(('grp', 'mem')), may hold values from -6 to 6
- projection: bfloat16 [2048, 2048], replicated, may hold values from -0.125 to 0.125
- item_table: bfloat16 [8192, 2048], P(('grp', 'mem')), may hold values from -8 to 8
- positive: int32 [16384], P(('grp', 'mem')), may hold values from 0 to 8191, as said below
- negatives: int32 [4, 1024], P(None, ('grp', 'mem')), may hold values from 0 to 8191, as said below
Outputs:
- user_grad: bfloat16 [16384, 2048], P(('grp', 'mem'))
- item_grad: float32 [8192, 2048], P(('grp', 'mem'))
Inputs may be any that keep to these rules, and one draw needn't show every extreme that they name: `positive`: owner o (grp-major order over grp and mem) holds item rows o * 64 to (o + 1) * 64 - 1. Among the 128 rows of any one device, at most 4 positives lie with any one owner, and one owner receives exactly 4 from every device. `negatives`: in every group, negative j is one of the item rows of owner j // 8.
All inputs are finite; a program needn't handle non-finite values.
Results may differ from a plain program's by a relative error of at most 0.0075.
Values may be sent and summed in bfloat16 or wider, within the bound.
A program may use at most 64 MiB of HBM per device.

v0:
```python
import math

import jax
import jax.numpy as jnp
from jax import lax
from jax.sharding import PartitionSpec as P


def select_rows(local_ids, item_block):
    onehot = (local_ids[..., None] == jnp.arange(item_block.shape[0], dtype=jnp.int32)).astype(
        item_block.dtype
    )
    return jnp.einsum(
        "...r,rd->...d", onehot, item_block, preferred_element_type=jnp.float32
    ).astype(item_block.dtype)


def collect_rows(local_ids, grad_rows, row_count):
    safe_ids = jnp.where(local_ids < 0, row_count, local_ids)
    totals = jnp.zeros((row_count, grad_rows.shape[1]), jnp.float32)
    return totals.at[safe_ids].add(grad_rows, mode="drop")


def silu_slope(hidden):
    sigmoid_value = jax.nn.sigmoid(hidden)
    return sigmoid_value * (1.0 + hidden * (1.0 - sigmoid_value))


def on_device(user_rows, projection, item_table, positive, negatives):
    rows_here, row_width = user_rows.shape
    own_rows = item_table.shape[0]
    owners = lax.axis_size("grp") * lax.axis_size("mem")
    capacity = 4 * rows_here // owners
    score_scale = 4.0 / math.sqrt(row_width)
    first_row = lax.axis_index(("grp", "mem")) * own_rows
    local_neg = negatives - first_row
    picked = select_rows(local_neg, item_table)
    arrived = lax.all_to_all(picked, "grp", split_axis=0, concat_axis=0, tiled=True)
    neg_table = lax.all_gather(arrived.reshape(-1, row_width), "mem", axis=0, tiled=True)
    hidden = jnp.dot(user_rows, projection, preferred_element_type=jnp.float32)
    hidden_z = jax.nn.silu(hidden).astype(jnp.bfloat16)
    owner_index = positive // own_rows
    offset = positive - owner_index * own_rows
    hit_table = (owner_index[:, None] == jnp.arange(owners, dtype=jnp.int32)).astype(jnp.int32)
    before = jnp.sum((jnp.cumsum(hit_table, axis=0) - hit_table) * hit_table, axis=1)
    slot_index = owner_index * capacity + before
    request = (
        jnp.full((owners * capacity,), -1, jnp.int32)
        .at[slot_index]
        .set(offset)
        .reshape(owners, capacity)
    )
    received = lax.all_to_all(request, ("grp", "mem"), split_axis=0, concat_axis=0, tiled=True)
    found_rows = select_rows(received, item_table)
    answers = lax.all_to_all(found_rows, ("grp", "mem"), split_axis=0, concat_axis=0, tiled=True)
    pos_rows = answers.reshape(owners * capacity, row_width)[slot_index]
    neg_logits = score_scale * jnp.einsum(
        "ud,nd->un", hidden_z, neg_table, preferred_element_type=jnp.float32
    )
    pos_logit = score_scale * jnp.sum(
        hidden_z.astype(jnp.float32) * pos_rows.astype(jnp.float32), axis=1
    )
    row_max = jnp.maximum(pos_logit, jnp.max(neg_logits, axis=1))
    exp_total = jnp.exp(pos_logit - row_max) + jnp.sum(
        jnp.exp(neg_logits - row_max[:, None]), axis=1
    )
    log_total = row_max + jnp.log(exp_total)
    neg_prob = jnp.exp(neg_logits - log_total[:, None]).astype(jnp.bfloat16)
    pos_weight = jnp.exp(pos_logit - log_total) - 1.0
    grad_z = score_scale * (
        jnp.dot(neg_prob, neg_table, preferred_element_type=jnp.float32)
        + pos_weight[:, None] * pos_rows.astype(jnp.float32)
    )
    grad_hidden = (grad_z * silu_slope(hidden)).astype(jnp.bfloat16)
    user_grad = jnp.einsum(
        "ue,de->ud", grad_hidden, projection, preferred_element_type=jnp.float32
    ).astype(jnp.bfloat16)
    share = lax.psum_scatter(
        (
            score_scale
            * jnp.einsum("un,ud->nd", neg_prob, hidden_z, preferred_element_type=jnp.float32)
        ).astype(jnp.bfloat16),
        "mem",
        scatter_dimension=0,
        tiled=True,
    ).astype(jnp.float32)
    returned = lax.all_to_all(
        share.reshape(arrived.shape[0], arrived.shape[1], row_width).astype(jnp.bfloat16),
        "grp",
        split_axis=0,
        concat_axis=0,
        tiled=True,
    ).astype(jnp.float32)
    item_grad = collect_rows(local_neg.reshape(-1), returned.reshape(-1, row_width), own_rows)
    pos_term = (score_scale * pos_weight)[:, None] * hidden_z.astype(jnp.float32)
    grad_slots = jnp.zeros((owners * capacity, row_width), jnp.float32).at[slot_index].set(pos_term)
    grad_rows = lax.all_to_all(
        grad_slots.reshape(owners, capacity, row_width).astype(jnp.bfloat16),
        ("grp", "mem"),
        split_axis=0,
        concat_axis=0,
        tiled=True,
    ).astype(jnp.float32)
    item_grad = item_grad + collect_rows(
        received.reshape(-1), grad_rows.reshape(-1, row_width), own_rows
    )
    return (user_grad, item_grad)


def solution(mesh):
    placed = (
        P(("grp", "mem"), None),
        P(),
        P(("grp", "mem"), None),
        P(("grp", "mem")),
        P(None, ("grp", "mem")),
    )
    return jax.shard_map(
        on_device,
        mesh=mesh,
        in_specs=placed,
        out_specs=(P(("grp", "mem"), None), P(("grp", "mem"), None)),
        check_vma=False,
    )
```

profile of v0, /device:TPU:0, one launch (start us, length us, event | category | flops | bytes accessed | tf_op | source)
XLA Modules:
  0.0 214.9 jit_solution(2081257013145953165)
XLA Ops:
  7.2 0.0 copy-start
  7.2 0.0 all-gather.2.cloned.1.call-start
  7.2 0.7 broadcast_subtract_fusion
  8.0 1.2 convolution_convert_fusion.2
  9.1 10.3 %all_to_all.29 = bf16[4,8,2048]{2,1,0:T(8,128)(2,1)} all-to-all(bf16[4,8,2048]{2,1,0:T(8,128)(2,1)S(1)} %convolution_convert_fusion.2), channel_id=1, replica_groups=mesh['grp'=4,'mem'=32] {'grp'}, dimensions={0} | all-to-all | bytes 262144 | tf_op jit(solution)/shard_map/all_to_all | solution.py:38
  19.4 0.0 all-gather.2.cloned.1.call-update
  19.4 0.7 multiply_subtract_fusion
  20.1 0.1 fusion.19
  20.2 0.2 reduce_window_sum.11
  20.4 0.2 select_reduce_fusion
  20.5 1.0 scatter_custom_fusion
  21.5 0.1 all_to_all.19
  21.6 18.3 %all_to_all.30 = s32[128,1,4]{2,1,0:T(1,128)S(1)} all-to-all(s32[128,1,4]{2,1,0:T(1,128)S(1)} %bitcast.29), channel_id=1, replica_groups=mesh['grp'=4,'mem'=32] {'grp','mem'}, dimensions={0} | all-to-all | bytes 4096 | tf_op jit(solution)/shard_map/all_to_all | solution.py:53
  40.0 0.1 copy.10
  40.0 1.7 convolution_convert_fusion
  41.8 3.0 %copy.11 = bf16[128,4,2048]{2,1,0:T(4,128)(2,1)} copy(bf16[128,4,2048]{2,0,1:T(8,128)(2,1)S(1)} %convolution_convert_fusion) | data formatting | bytes 4194304 | tf_op jit(solution)/shard_map/convert_element_type | solution.py:15
  44.7 5.8 %all-to-all-start.2 = ((bf16[128,4,2048]{2,1,0:T(4,128)(2,1)}), bf16[128,4,2048]{2,1,0:T(4,128)(2,1)}, u32[]{:S(2)}, u32[]{:S(2)}) async-start(bf16[128,4,2048]{2,1,0:T(4,128)(2,1)} %copy.11), calls=%async_computation.2 | async-start | bytes 4194304 | tf_op jit(solution)/shard_map/all_to_all | solution.py:55
  50.5 0.0 reduce-scatter.2.cloned.1.call-start
  50.6 30.0 %all-to-all-done.2 = bf16[128,4,2048]{2,1,0:T(4,128)(2,1)} async-done(((bf16[128,4,2048]{2,1,0:T(4,128)(2,1)}), bf16[128,4,2048]{2,1,0:T(4,128)(2,1)}, u32[]{:S(2)}, u32[]{:S(2)}) %all-to-all-start.2) | async-done | bytes 2097184 | tf_op jit(solution)/shard_map/all_to_all | solution.py:55
  80.6 2.6 %reshape.131 = bf16[512,2048]{1,0:T(8,128)(2,1)S(1)} reshape(bf16[128,4,2048]{2,1,0:T(4,128)(2,1)} %all-to-all-done.2) | data formatting | bytes 4194304 | tf_op jit(solution)/shard_map/reshape | solution.py:56
  83.2 0.9 gather_fusion
  84.1 0.0 copy-done
  84.1 0.0 copy-start.1
  84.1 6.2 %fusion.5 = (f32[128]{0:T(128)S(1)}, bf16[128,2048]{1,0:T(8,128)(2,1)S(1)}, f32[128,2048]{1,0:T(8,128)}) fusion(bf16[128,2048]{1,0:T(8,128)(2,1)S(1)} %gather_fusion, bf16[128,2048]{1,0:T(8,128)(2,1)S(1)} %copy-done, bf16[2048,2048]{1,0:T(8,128)(2,1)} %param.6), kind=kOutput, calls=%fused_computation.19 | convolution fusion | flops 1076100992 | bytes 11010560 | tf_op jit(solution)/shard_map/dot_general | solution.py:40
  90.3 0.0 copy-done.1
  90.3 0.0 all-gather.2.cloned.1.call-done
  90.3 3.8 %fusion.27 = (f32[128]{0:T(128)S(1)}, f32[128,1024]{1,0:T(8,128)S(1)}) fusion(bf16[128,2048]{1,0:T(8,128)(2,1)S(1)} %get-tuple-element.6, bf16[1024,2048]{1,0:T(8,128)(2,1)} %all-gather.2.cloned.1.call-done), kind=kOutput, calls=%fused_computation.65 | convolution fusion | flops 537132928 | bytes 5243392 | tf_op jit(solution)/shard_map/ud,nd->un/dot_general | solution.py:57
  94.1 0.2 exponential_reduce_fusion
  94.4 3.3 %multiply_convert_fusion = bf16[1024,2048]{1,0:T(8,128)(2,1)} fusion(bf16[128,2048]{1,0:T(8,128)(2,1)S(1)} %get-tuple-element.6, f32[128,1024]{1,0:T(8,128)S(1)} %get-tuple-element.11, f32[128]{0:T(128)S(1)} %get-tuple-element.4), kind=kOutput, calls=%fused_computation.5 | convolution fusion | flops 541327360 | bytes 5243392 | tf_op jit(solution)/shard_map/un,ud->nd/dot_general | solution.py:81
  97.7 0.0 reduce-scatter.2.cloned.1.call-update
  97.7 3.5 %scatter_custom_fusion.2 = f32[512,2048]{1,0:T(8,128)} fusion(s32[128]{0:T(128)S(1)} %compare_select_fusion.4, f32[]{:T(128)} %constant.59.clone.1, bf16[128,2048]{1,0:T(8,128)(2,1)S(1)} %get-tuple-element.6, f32[128]{0:T(128)S(1)} %get-tuple-element.2), kind=kCustom, calls=%fused_computation.13 | custom fusion | flops 524288 | bytes 4719108 | tf_op jit(solution)/shard_map/scatter | solution.py:96
  101.3 2.5 %convert_element_type.58 = bf16[512,2048]{1,0:T(8,128)(2,1)S(1)} convert(f32[512,2048]{1,0:T(8,128)} %scatter_custom_fusion.2) | non-fusion elementwise | flops 1048576 | bytes 6291456 | tf_op jit(solution)/shard_map/convert_element_type | solution.py:98
  103.8 2.3 %convert_element_type.59 = bf16[128,4,2048]{2,1,0:T(4,128)(2,1)} reshape(bf16[512,2048]{1,0:T(8,128)(2,1)S(1)} %convert_element_type.58) | data formatting | bytes 4194304 | tf_op jit(solution)/shard_map/convert_element_type | solution.py:98
  106.0 9.8 %all-to-all-start.4 = ((bf16[128,4,2048]{2,1,0:T(4,128)(2,1)}), bf16[128,4,2048]{2,1,0:T(4,128)(2,1)S(1)}, u32[]{:S(2)}, u32[]{:S(2)}) async-start(bf16[128,4,2048]{2,1,0:T(4,128)(2,1)} %convert_element_type.59), calls=%async_computation.5 | async-start | bytes 4194304 | tf_op jit(solution)/shard_map/all_to_all | solution.py:97
  115.9 0.1 reshape.132
  115.9 0.5 broadcast.150
  116.5 0.8 reduce.3
  117.3 0.1 reshape.135
  117.4 28.7 %all-to-all-done.4 = bf16[128,4,2048]{2,1,0:T(4,128)(2,1)S(1)} async-done(((bf16[128,4,2048]{2,1,0:T(4,128)(2,1)}), bf16[128,4,2048]{2,1,0:T(4,128)(2,1)S(1)}, u32[]{:S(2)}, u32[]{:S(2)}) %all-to-all-start.4) | async-done | bytes 2097184 | tf_op jit(solution)/shard_map/all_to_all | solution.py:97
  146.1 34.8 %reduce-scatter.2.cloned.1.call-done = bf16[32,2048]{1,0:T(8,128)(2,1)} async-done(((bf16[1024,2048]{1,0:T(8,128)(2,1)}), bf16[32,2048]{1,0:T(8,128)(2,1)}) %reduce-scatter.2.cloned.1.call-update) | async-done | bytes 131088 | tf_op jit(solution)/shard_map/reduce_scatter | solution.py:78
  180.9 4.3 %all-to-all-start.3 = ((bf16[4,8,2048]{2,1,0:T(8,128)(2,1)}), bf16[4,8,2048]{2,1,0:T(8,128)(2,1)S(1)}, u32[]{:S(2)}, u32[]{:S(2)}) async-start(bf16[4,8,2048]{2,1,0:T(8,128)(2,1)} %bitcast.30), calls=%async_computation.4 | async-start | bytes 262144 | tf_op jit(solution)/shard_map/all_to_all | solution.py:87
  185.2 9.8 %convolution_convert_fusion.1 = bf16[128,2048]{1,0:T(8,128)(2,1)} fusion(bf16[2048,2048]{1,0:T(8,128)(2,1)} %param.6, bf16[1024,2048]{1,0:T(8,128)(2,1)} %all-gather.2.cloned.1.call-done, bf16[128,2048]{1,0:T(8,128)(2,1)} %copy-done.1, f32[128,2048]{1,0:T(8,128)} %get-tuple-element.9, f32[128]{0:T(128)S(1)} %get-tuple-element.3, ...), kind=kOutput, calls=%fused_computation.11 | convolution fusion | flops 1614544896 | bytes 15205376 | tf_op jit(solution)/shard_map/ue,de->ud/dot_general | solution.py:75
  195.0 2.5 %reshape.178 = f32[512,2048]{1,0:T(8,128)} reshape(bf16[128,4,2048]{2,1,0:T(4,128)(2,1)S(1)} %all-to-all-done.4) | data formatting | bytes 6291456 | tf_op jit(solution)/shard_map/reshape | solution.py:105
  197.5 8.6 %scatter_custom_fusion.3 = f32[64,2048]{1,0:T(8,128)S(1)} fusion(s32[512]{0:T(512)S(1)} %bitcast.31, f32[512,2048]{1,0:T(8,128)} %reshape.178, f32[]{:T(128)} %constant.59.clone.1), kind=kCustom, calls=%fused_computation.32 | custom fusion | flops 1048576 | bytes 524800 | tf_op jit(solution)/shard_map/scatter-add | solution.py:21
  206.1 0.0 all-to-all-done.3
  206.1 1.1 scatter_custom_fusion.1
  207.2 0.9 add.98
  (6 shorter events, 0.1 us)
Async XLA Ops:
  7.2 77.0 %copy-start = (bf16[128,2048]{1,0:T(8,128)(2,1)S(1)}, bf16[128,2048]{1,0:T(8,128)(2,1)}, u32[]{:S(2)}) copy-start(bf16[128,2048]{1,0:T(8,128)(2,1)} %param.5) | copy-start | bytes 1572868
  7.2 83.1 %all-gather.2.cloned.1.call-start = ((), (), s32[]{:S(2)}) async-start(), calls=%async_computation.6 | async-start | bytes 4325376 | tf_op jit(solution)/shard_map/all_gather | solution.py:39
  44.7 35.8 %all-to-all-start.2 = ((bf16[128,4,2048]{2,1,0:T(4,128)(2,1)}), bf16[128,4,2048]{2,1,0:T(4,128)(2,1)}, u32[]{:S(2)}, u32[]{:S(2)}) async-start(bf16[128,4,2048]{2,1,0:T(4,128)(2,1)} %copy.11), calls=%async_computation.2 | async-start | bytes 4194304 | tf_op jit(solution)/shard_map/all_to_all | solution.py:55
  50.5 130.4 %reduce-scatter.2.cloned.1.call-start = ((), (), s32[]{:S(2)}) async-start(), calls=%async_computation.7 | async-start | bytes 4325376 | tf_op jit(solution)/shard_map/reduce_scatter | solution.py:78
  84.1 6.2 %copy-start.1 = (bf16[128,2048]{1,0:T(8,128)(2,1)}, bf16[128,2048]{1,0:T(8,128)(2,1)S(1)}, u32[]{:S(2)}) copy-start(bf16[128,2048]{1,0:T(8,128)(2,1)S(1)} %gather_fusion) | copy-start | bytes 1572868
  106.0 40.1 %all-to-all-start.4 = ((bf16[128,4,2048]{2,1,0:T(4,128)(2,1)}), bf16[128,4,2048]{2,1,0:T(4,128)(2,1)S(1)}, u32[]{:S(2)}, u32[]{:S(2)}) async-start(bf16[128,4,2048]{2,1,0:T(4,128)(2,1)} %convert_element_type.59), calls=%async_computation.5 | async-start | bytes 4194304 | tf_op jit(solution)/shard_map/all_to_all | solution.py:97
  180.9 25.1 %all-to-all-start.3 = ((bf16[4,8,2048]{2,1,0:T(8,128)(2,1)}), bf16[4,8,2048]{2,1,0:T(8,128)(2,1)S(1)}, u32[]{:S(2)}, u32[]{:S(2)}) async-start(bf16[4,8,2048]{2,1,0:T(8,128)(2,1)} %bitcast.30), calls=%async_computation.4 | async-start | bytes 262144 | tf_op jit(solution)/shard_map/all_to_all | solution.py:87
Sparse Core Ops, SparseCore 0:
  19.5 68.5 all-gather.1
  97.8 83.0 reduce-scatter.1
where the time goes:
time: 216 us; the launch traced here: 215 us
  waiting for transfers between devices  93.5 us (43%)
  blocking collectives  28.6 us (13%)
  matrix products  26 us (12%)
  starting transfers between devices  19.9 us (9%)
  other arithmetic  19.5 us (9%)
  between operations  14.2 us (7%)
  local copies, waits for them, and re-layouts  13.1 us (6%)
    reduce_scatter x1, waiting for transfers between devices, on_device(): lax.psum_scatter((score_scale * jnp.einsum('un,ud->nd', neg_prob, hidden_...  34.8 us
    all_to_all x1, waiting for transfers between devices, on_device(): lax.all_to_all(found_rows, ('grp', 'mem'), split_axis=0, concat_axis=0, t...  30 us
    all_to_all x1, waiting for transfers between devices, on_device(): lax.all_to_all(grad_slots.reshape(owners, capacity, row_width).astype(jnp...  28.7 us
    all_to_all x1, blocking collectives, on_device(): lax.all_to_all(request, ('grp', 'mem'), split_axis=0, concat_axis=0, tile...  18.3 us
    all_to_all x1, blocking collectives, on_device(): lax.all_to_all(picked, 'grp', split_axis=0, concat_axis=0, tiled=True)  10.3 us
    dot_general x1, matrix products, on_device(): jnp.einsum('ue,de->ud', grad_hidden, projection, preferred_element_type=j...  9.82 us
    all_to_all x1, starting transfers between devices, on_device(): lax.all_to_all(grad_slots.reshape(owners, capacity, row_width).astype(jnp...  9.8 us
    scatter-add x2, other arithmetic, collect_rows(): return totals.at[safe_ids].add(grad_rows, mode='drop')  9.69 us
  transfers between devices with their start and end apart: 5, of which 3 were waited for; matrix products, arithmetic and copies ran while one was open for 22% of the time, Pallas kernels for 0%

commit v1 on v0

v1 whole, which is shorter than its diff:
```python
import functools
import math

import jax
import jax.numpy as jnp
from jax import lax
from jax.experimental import pallas as pl
from jax.experimental.pallas import tpu as pltpu
from jax.sharding import PartitionSpec as P

MESH = pl.DeviceIdType.MESH
BF, F32, I32 = jnp.bfloat16, jnp.float32, jnp.int32
W = 2048
HALF = W // 2
CH = 512
NC = W // CH
ROWS = 64
USERS = 128
SLOTS = 16
RING = (0, 1, -1, 2)
PLACE = {0: 0, 1: 1, -1: 2, 2: 3}
FULL, LEFT, RIGHT = pl.ds(0, W), pl.ds(0, HALF), pl.ds(HALF, HALF)


def fold(v):
    return {-3: 1, -2: 2, 3: -1}.get(v, v)


def dot(a, b, ca=1, cb=0):
    return lax.dot_general(a, b, (((ca,), (cb,)), ((), ())), preferred_element_type=F32)


def kernel(
    user_hbm, proj_hbm, tab, pos_lane, pos_col, neg_col, neg_lane, ug_ref, ig_ref,
    users, proj, hidden, z_ref, gh, probs, logits, pos_rows,
    shards, table, ids, pick_ref, slot_of, slot_to, send_slots, recv_slots, send_grads, recv_grads,
    back, back_in, xs, xr, part, sib_in, r_left, r_right, r_a, r_b,
    load_sem, ids_sem, shard_sem, slot_sem, grad_sem, back_sem, x_sem,
    ag_send, ag_recv, sib_send, sib_recv, rs_send, rs_recv,
):
    scale = 4.0 / math.sqrt(W)
    g, m = lax.axis_index("grp"), lax.axis_index("mem")
    c, y, zz = lax.rem(m, 2), lax.rem(m // 2, 4), m // 8
    me = (g * 4 + zz) * 2 + c

    def dev(gx, dz, dy, cc):
        return (gx, (lax.rem(zz + dz + 4, 4) * 4 + lax.rem(y + dy + 4, 4)) * 2 + cc)

    def mate(i):
        u = lax.rem(me + i, 32)
        return u, (u // 8, (lax.rem(u // 2, 4) * 4 + y) * 2 + lax.rem(u, 2))

    def xpeer(i):
        gx = lax.rem(g + i, 4)
        return gx, (gx, m)

    sib = dev(g, 0, 0, 1 - c)
    late = []

    def remote(src, dst, s_sem, r_sem, to):
        cp = pltpu.make_async_remote_copy(
            src_ref=src, dst_ref=dst, send_sem=s_sem, recv_sem=r_sem, device_id=to, device_id_type=MESH
        )
        cp.start()
        return cp

    def arrive(ref, sem):
        pltpu.make_async_copy(ref, ref, sem).wait()

    barrier = pltpu.get_barrier_semaphore()

    def greet(i, carry):
        pl.semaphore_signal(barrier, inc=1, device_id=mate(i)[1], device_id_type=MESH)
        return carry

    lax.fori_loop(1, 32, greet, 0)
    for dy in (1, 2, 3):
        pl.semaphore_signal(barrier, inc=1, device_id=dev(g, 0, dy, c), device_id_type=MESH)

    loads = [pltpu.make_async_copy(user_hbm, users, load_sem.at[0])]
    for t in range(NC):
        cols = pl.ds(t * CH, CH)
        loads.append(pltpu.make_async_copy(proj_hbm.at[:, cols], proj.at[:, cols], load_sem.at[1 + t]))
    for cp in loads:
        cp.start()

    pick = (neg_col[...] == lax.broadcasted_iota(I32, (32, ROWS), 1)).astype(BF)
    picked = dot(pick, tab[...])
    for gi in range(4):
        rows8 = picked[8 * gi:8 * gi + 8, :]
        xs[gi] = jnp.concatenate([rows8[:, :HALF], rows8[:, HALF:]], axis=0).astype(BF)
    my_shard = pl.ds(pl.multiple_of(y * ROWS, ROWS), ROWS)
    shards[my_shard, :] = tab[...]
    ids[me] = pos_lane[...]
    pl.semaphore_wait(barrier, 34)

    for i in (1, 2, 3):
        gx, to = xpeer(i)
        late.append(remote(xs.at[gx], xr.at[g], x_sem.at[0], x_sem.at[1], to))
    xr[g] = xs[g]

    def send_ids(i, carry):
        remote(pos_lane, ids.at[me], ids_sem.at[0], ids_sem.at[1], mate(i)[1])
        return carry

    lax.fori_loop(1, 32, send_ids, 0)
    for t in range(NC):
        for dy in (1, 3, 2):
            cols = pl.ds(t * CH, CH)
            remote(tab.at[:, cols], shards.at[my_shard, cols], shard_sem.at[0, t], shard_sem.at[1, t], dev(g, 0, dy, c))

    def block(cc, dz, dy):
        at = ((cc * 4 + lax.rem(zz + dz + 4, 4)) * 4 + lax.rem(y + dy + 4, 4)) * 32
        return pl.ds(pl.multiple_of(at, 32), 32)

    def sem_at(f, s, p):
        return (PLACE[f] * 4 + PLACE[s]) * 2 + p

    count = [0]

    def push(f, s, cols, along_z, sgn, p):
        nf, ns = (fold(f - sgn), s) if along_z else (f, fold(s - sgn))
        ref = table.at[block(c, f, s), cols]
        to = dev(g, sgn, 0, c) if along_z else dev(g, 0, sgn, c)
        late.append(remote(ref, ref, ag_send.at[count[0]], ag_recv.at[sem_at(nf, ns, p)], to))
        count[0] += 1

    across = []

    def over(f, s, cols, p):
        ref = table.at[block(c, f, s), cols]
        k = sem_at(f, s, p)
        late.append(remote(ref, ref, sib_send.at[k], sib_recv.at[k], sib))
        across.append((f, s, cols, p))

    def here(f, s, cols, p):
        arrive(table.at[block(c, f, s), cols], ag_recv.at[sem_at(f, s, p)])

    def second(f, cols, p):
        push(f, 0, cols, False, 1, p)
        push(f, 0, cols, False, -1, p)
        over(f, 0, cols, p)

    def relay(f, parts):
        for cols, p in parts:
            for s in (-1, 1):
                here(f, s, cols, p)
                over(f, s, cols, p)
        push(f, -1, LEFT, False, 1, 0)
        push(f, 1, RIGHT, False, -1, 1)

    arrive(xr.at[pl.ds(0, 3)], x_sem.at[1])
    lines = []
    for gi in range(4):
        v = xr[gi].astype(F32)
        lines.append(jnp.concatenate([v[:8], v[8:]], axis=1))
    table[block(c, 0, 0), :] = jnp.concatenate(lines, axis=0).astype(BF)
    push(0, 0, FULL, True, 1, 0)
    push(0, 0, FULL, True, -1, 0)
    second(0, FULL, 0)

    lane = lax.broadcasted_iota(I32, (USERS, USERS), 1)
    sub = lax.broadcasted_iota(I32, (USERS, USERS), 0)
    own_c, own_l = pos_col[...] >> 6, pos_lane[...] >> 6
    same = own_c == own_l
    rank_c = jnp.sum((same & (lane < sub)).astype(F32), axis=1, keepdims=True).astype(I32)
    rank_l = jnp.sum((same & (sub < lane)).astype(F32), axis=0, keepdims=True).astype(I32)

    def slot(o, rank):
        relay_of = ((o >> 5) * 4 + ((o >> 3) & 3)) * 2 + (o & 1)
        return relay_of * SLOTS + ((o >> 1) & 3) * 4 + rank

    slot_of[...] = (slot(own_c, rank_c) == lax.broadcasted_iota(I32, (USERS, 512), 1)).astype(BF)
    slot_to[...] = (slot(own_l, rank_l) == lax.broadcasted_iota(I32, (512, USERS), 0)).astype(BF)

    arrive(ids.at[pl.ds(0, 31)], ids_sem.at[1])
    wide = jnp.broadcast_to(ids[...], (32, SLOTS, USERS)).reshape(512, USERS)
    s_iota = lax.broadcasted_iota(I32, (512, USERS), 0) & (SLOTS - 1)
    owner_q = g * 32 + (zz * 4 + (s_iota >> 2)) * 2 + c
    hit = (wide >> 6) == owner_q
    before = dot(hit.astype(BF), (sub < lane).astype(BF))
    take = hit & (before == (s_iota & 3).astype(F32))
    found = jnp.sum(jnp.where(take, (wide & 63) + 1, 0).astype(F32), axis=1, keepdims=True).astype(I32)
    q_col = (lax.broadcasted_iota(I32, (512, 1), 0) & (SLOTS - 1)) >> 2
    target = jnp.where(found > 0, q_col * ROWS + found - 1, -1)
    pick_ref[...] = (target == lax.broadcasted_iota(I32, (512, 256), 1)).astype(BF)

    def my_slots(u):
        return pl.ds(pl.multiple_of(u * SLOTS, SLOTS), SLOTS)

    def gather(t):
        cols = pl.ds(t * CH, CH)
        arrive(shards.at[pl.ds(0, 192), cols], shard_sem.at[1, t])
        send_slots[:, cols] = dot(pick_ref[...], shards[:, cols]).astype(BF)

        def out(i, carry):
            u, to = mate(i)
            remote(send_slots.at[my_slots(u), cols], recv_slots.at[my_slots(me), cols], slot_sem.at[0, t], slot_sem.at[1, t], to)
            return carry

        lax.fori_loop(1, 32, out, 0)
        recv_slots[my_slots(me), cols] = send_slots[my_slots(me), cols]

    def project(t):
        cols = pl.ds(t * CH, CH)
        loads[1 + t].wait()
        h = dot(users[...], proj[:, cols])
        hidden[:, cols] = h
        z_ref[:, cols] = (h * jax.nn.sigmoid(h)).astype(BF)

    here(-1, 0, FULL, 0)
    push(-1, 0, LEFT, True, 1, 0)
    here(1, 0, FULL, 0)
    push(1, 0, RIGHT, True, -1, 1)
    second(-1, FULL, 0)
    second(1, FULL, 0)
    gather(0)
    relay(0, [(FULL, 0)])
    gather(1)
    here(2, 0, LEFT, 0)
    second(2, LEFT, 0)
    here(2, 0, RIGHT, 1)
    second(2, RIGHT, 1)
    loads[0].wait()
    project(0)
    gather(2)
    relay(-1, [(FULL, 0)])
    project(1)
    relay(1, [(FULL, 0)])
    gather(3)
    project(2)
    relay(2, [(LEFT, 0), (RIGHT, 1)])
    project(3)
    for f in RING:
        here(f, 2, LEFT, 0)
        over(f, 2, LEFT, 0)
        here(f, 2, RIGHT, 1)
        over(f, 2, RIGHT, 1)

    def log_rows(cc):
        for t in range(2):
            rows = pl.ds(pl.multiple_of(cc * 512 + t * 256, 256), 256)
            logits[:, rows] = scale * dot(z_ref[...], table[rows, :], 1, 1)

    log_rows(c)
    for f, s, cols, p in across:
        arrive(table.at[block(1 - c, f, s), cols], sib_recv.at[sem_at(f, s, p)])
    log_rows(1 - c)
    pos_logit = jnp.zeros((USERS, 1), F32)
    for t in range(NC):
        cols = pl.ds(t * CH, CH)
        arrive(recv_slots.at[pl.ds(0, 31 * SLOTS), cols], slot_sem.at[1, t])
        pr = dot(slot_of[...], recv_slots[:, cols])
        pos_rows[:, cols] = pr
        pos_logit = pos_logit + jnp.sum(z_ref[:, cols].astype(F32) * pr, axis=1, keepdims=True)
    pos_logit = scale * pos_logit
    lg = logits[...]
    top = jnp.maximum(pos_logit, jnp.max(lg, axis=1, keepdims=True))
    total = jnp.exp(pos_logit - top) + jnp.sum(jnp.exp(lg - top), axis=1, keepdims=True)
    log_total = top + jnp.log(total)
    probs[...] = jnp.exp(lg - log_total).astype(BF)
    pos_weight = jnp.exp(pos_logit - log_total) - 1.0

    for t in range(NC):
        cols = pl.ds(t * CH, CH)
        term = ((scale * pos_weight) * z_ref[:, cols].astype(F32)).astype(BF)
        send_grads[:, cols] = dot(slot_to[...], term).astype(BF)

        def out(i, carry, cols=cols, t=t):
            u, to = mate(i)
            remote(send_grads.at[my_slots(u), cols], recv_grads.at[my_slots(me), cols], grad_sem.at[0, t], grad_sem.at[1, t], to)
            return carry

        lax.fori_loop(1, 32, out, 0)
        recv_grads[my_slots(me), cols] = send_grads[my_slots(me), cols]

    def line(cc, dz):
        return pl.ds(pl.multiple_of((cc * 4 + lax.rem(zz + dz + 4, 4)) * 128, 128), 128)

    ORDER = (2, 1, -1, 0)
    for i, dz in enumerate(ORDER):
        for cc in (1 - c, c):
            rows = line(cc, dz)
            pt = probs[:, rows]
            for t in range(NC):
                cols = pl.ds(t * CH, CH)
                part[rows, cols] = (scale * dot(pt, z_ref[:, cols], 0, 0)).astype(BF)
        late.append(remote(part.at[line(1 - c, dz)], sib_in.at[i], rs_send.at[i], rs_recv.at[i], sib))

    rs_count = [4]

    def push_sum(src, dst, k, to):
        late.append(remote(src, dst, rs_send.at[rs_count[0]], rs_recv.at[k], to))
        rs_count[0] += 1

    def ring(i, rows, to):
        def first():
            push_sum(part.at[rows(2), LEFT], r_left.at[i], 4 + 4 * i, to(-1))
            push_sum(part.at[rows(2), RIGHT], r_right.at[i], 5 + 4 * i, to(1))

        def middle():
            arrive(r_left.at[i], rs_recv.at[4 + 4 * i])
            r = rows(-1)
            part[r, LEFT] = (part[r, LEFT].astype(F32) + r_left[i].astype(F32)).astype(BF)
            push_sum(part.at[r], r_a.at[i], 6 + 4 * i, to(-1))
            arrive(r_right.at[i], rs_recv.at[5 + 4 * i])
            r = rows(1)
            part[r, RIGHT] = (part[r, RIGHT].astype(F32) + r_right[i].astype(F32)).astype(BF)
            push_sum(part.at[r], r_b.at[i], 7 + 4 * i, to(1))

        def last():
            arrive(r_a.at[i], rs_recv.at[6 + 4 * i])
            arrive(r_b.at[i], rs_recv.at[7 + 4 * i])
            r = rows(0)
            return part[r, :].astype(F32) + r_a[i].astype(F32) + r_b[i].astype(F32)

        return first, middle, last

    rings = []
    for i, dz in enumerate(ORDER):
        arrive(sib_in.at[i], rs_recv.at[i])
        rows = line(c, dz)
        part[rows, :] = (part[rows, :].astype(F32) + sib_in[i].astype(F32)).astype(BF)
        rings.append(ring(i, lambda d, dz=dz: block(c, dz, d), lambda s: dev(g, 0, s, c)))
        rings[i][0]()

    def slope(t):
        cols = pl.ds(t * CH, CH)
        h = hidden[:, cols]
        sg = jax.nn.sigmoid(h)
        gz = scale * (dot(probs[...], table[:, cols]) + pos_weight * pos_rows[:, cols])
        gh[:, cols] = (gz * (sg * (1.0 + h * (1.0 - sg)))).astype(BF)

    def user(t):
        rows = pl.ds(t * CH, CH)
        ug_ref[:, rows] = dot(gh[...], proj[rows, :], 1, 1).astype(BF)

    def gather_back(t):
        cols = pl.ds(t * CH, CH)
        arrive(recv_grads.at[pl.ds(0, 31 * SLOTS), cols], grad_sem.at[1, t])
        back[:, cols] = dot(pick_ref[...], recv_grads[:, cols], 0, 0).astype(BF)
        for dy in (1, 3, 2):
            src = pl.ds(pl.multiple_of(lax.rem(y + dy, 4) * ROWS, ROWS), ROWS)
            remote(back.at[src, cols], back_in.at[my_shard, cols], back_sem.at[0, t], back_sem.at[1, t], dev(g, 0, dy, c))
        back_in[my_shard, cols] = back[my_shard, cols]

    slope(0)
    rings[0][1]()
    slope(1)
    rings[1][1]()
    slope(2)
    rings[2][1]()
    slope(3)
    rings[3][1]()
    gather_back(0)
    lineup = ring(4, lambda d: block(c, d, 0), lambda s: dev(g, s, 0, c))

    def settle(i):
        part[block(c, ORDER[i], 0), :] = rings[i][2]().astype(BF)

    settle(0)
    lineup[0]()
    user(0)
    settle(1)
    settle(2)
    gather_back(1)
    lineup[1]()
    user(1)
    gather_back(2)
    mine = rings[3][2]()
    part[block(c, 0, 0), :] = mine.astype(BF)
    share = lineup[2]()
    for gi in range(4):
        rows8 = share[8 * gi:8 * gi + 8, :]
        xs[4 + gi] = jnp.concatenate([rows8[:, :HALF], rows8[:, HALF:]], axis=0).astype(BF)
    for i in (1, 2, 3):
        gx, to = xpeer(i)
        late.append(remote(xs.at[4 + gx], xr.at[4 + g], x_sem.at[2], x_sem.at[3], to))
    xr[4 + g] = xs[4 + g]
    gather_back(3)
    user(2)
    user(3)
    arrive(xr.at[pl.ds(4, 3)], x_sem.at[3])
    lines = []
    for gi in range(4):
        v = xr[4 + gi].astype(F32)
        lines.append(jnp.concatenate([v[:8], v[8:]], axis=1))
    returned = jnp.concatenate(lines, axis=0).astype(BF)
    place = (neg_lane[...] == lax.broadcasted_iota(I32, (ROWS, 32), 0)).astype(BF)
    for t in range(NC):
        cols = pl.ds(t * CH, CH)
        arrive(back_in.at[pl.ds(0, 192), cols], back_sem.at[1, t])
        acc = dot(place, returned[:, t * CH:(t + 1) * CH])
        for q in range(4):
            acc = acc + back_in[pl.ds(q * ROWS, ROWS), cols].astype(F32)
        ig_ref[:, cols] = acc

    for cp in late[:3]:
        pass
    arrive(xs.at[pl.ds(0, 3)], x_sem.at[0])
    arrive(xs.at[pl.ds(4, 3)], x_sem.at[2])
    arrive(ids.at[pl.ds(0, 31)], ids_sem.at[0])
    for t in range(NC):
        cols = pl.ds(t * CH, CH)
        arrive(shards.at[pl.ds(0, 192), cols], shard_sem.at[0, t])
        arrive(send_slots.at[pl.ds(0, 31 * SLOTS), cols], slot_sem.at[0, t])
        arrive(send_grads.at[pl.ds(0, 31 * SLOTS), cols], grad_sem.at[0, t])
        arrive(back.at[pl.ds(0, 192), cols], back_sem.at[0, t])
    for cp in late[3:-3]:
        cp.wait_send()


def on_device(user_rows, projection, item_table, positive, negatives):
    first_row = lax.axis_index(("grp", "mem")) * ROWS
    local = negatives - first_row
    vm = pl.BlockSpec(memory_space=pltpu.VMEM)
    hbm = pl.BlockSpec(memory_space=pl.ANY)
    dma = pltpu.SemaphoreType.DMA
    v = pltpu.VMEM
    return pl.pallas_call(
        kernel,
        out_shape=(jax.ShapeDtypeStruct((USERS, W), BF), jax.ShapeDtypeStruct((ROWS, W), F32)),
        in_specs=[hbm, hbm, vm, vm, vm, vm, vm],
        out_specs=(vm, vm),
        scratch_shapes=[
            v((USERS, W), BF), v((W, W), BF), v((USERS, W), F32), v((USERS, W), BF), v((USERS, W), BF),
            v((USERS, 1024), BF), v((USERS, 1024), F32), v((USERS, W), F32),
            v((256, W), BF), v((1024, W), BF), v((32, 1, USERS), I32), v((512, 256), BF),
            v((USERS, 512), BF), v((512, USERS), BF),
            v((512, W), BF), v((512, W), BF), v((512, W), BF), v((512, W), BF),
            v((256, W), BF), v((256, W), BF), v((8, 16, HALF), BF), v((8, 16, HALF), BF),
            v((1024, W), BF), v((4, 128, W), BF),
            v((5, 32, HALF), BF), v((5, 32, HALF), BF), v((5, 32, W), BF), v((5, 32, W), BF),
            dma((5,)), dma((2,)), dma((2, NC)), dma((2, NC)), dma((2, NC)), dma((2, NC)), dma((4,)),
            dma((40,)), dma((32,)), dma((32,)), dma((32,)), dma((24,)), dma((24,)),
        ],
        compiler_params=pltpu.CompilerParams(collective_id=0, has_side_effects=True, vmem_limit_bytes=58 << 20),
        cost_estimate=pl.CostEstimate(flops=5 * 10**9, bytes_accessed=12 * 2**20, transcendentals=10**6),
    )(
        user_rows,
        projection,
        item_table,
        positive.reshape(1, USERS),
        positive.reshape(USERS, 1),
        local.reshape(32, 1),
        local.reshape(1, 32),
    )


def solution(mesh):
    placed = (
        P(("grp", "mem"), None),
        P(),
        P(("grp", "mem"), None),
        P(("grp", "mem")),
        P(None, ("grp", "mem")),
    )
    return jax.shard_map(
        on_device,
        mesh=mesh,
        in_specs=placed,
        out_specs=(P(("grp", "mem"), None), P(("grp", "mem"), None)),
        check_vma=False,
    )
```

time: 216 us -> 96 us (0.44)
  waiting for transfers between devices: 93.5 us -> 0 us
  Pallas kernels: 0 us -> 88 us
  blocking collectives: 28.6 us -> 0 us
  matrix products: 26 us -> 0 us
  starting transfers between devices: 19.9 us -> 0 us
  other arithmetic: 19.5 us -> 0.69 us
  between operations: 14.2 us -> 0.65 us
  local copies, waits for them, and re-layouts: 13.1 us -> 6.42 us
    pallas_call x0 -> x1, Pallas kernels: none -> 88 us  [on_device(): pl.pallas_call(kernel, out_shape=(jax.ShapeDtypeStruct((USERS, W), BF), j...]
    all_to_all x3 -> x0, waiting for transfers between devices: 58.7 us -> none  [the longest x1 30 us: on_device(): lax.all_to_all(found_rows, ('grp', 'mem'), split_axis=0, concat_axis=0, t...]
    reduce_scatter x1 -> x0, waiting for transfers between devices: 34.8 us -> none  [on_device(): lax.psum_scatter((score_scale * jnp.einsum('un,ud->nd', neg_prob, hidden_...]
    all_to_all x2 -> x0, blocking collectives: 28.6 us -> none  [the longest x1 18.3 us: on_device(): lax.all_to_all(request, ('grp', 'mem'), split_axis=0, concat_axis=0, tile...]
    dot_general x6 -> x0, matrix products: 26 us -> none  [the longest x1 9.82 us: on_device(): jnp.einsum('ue,de->ud', grad_hidden, projection, preferred_element_type=j...]
    all_to_all x3 -> x0, starting transfers between devices: 19.8 us -> none  [the longest x1 9.8 us: on_device(): lax.all_to_all(grad_slots.reshape(owners, capacity, row_width).astype(jnp...]
    scatter-add x2 -> x0, other arithmetic: 9.69 us -> none  [collect_rows(): return totals.at[safe_ids].add(grad_rows, mode='drop')]
    convert_element_type x2 -> x0, local copies, waits for them, and re-layouts: 5.24 us -> none  [the longest x1 2.96 us: select_rows(): return jnp.einsum('...r,rd->...d', onehot, item_block, preferred_element_...]
  transfers between devices with their start and end apart: 5 -> 0, of which waited for: 3 -> 0; matrix products, arithmetic and copies ran while one was open for 22% -> 0% of each run, Pallas kernels for 0% -> 0%
where the time goes in v1:
time: 96 us; the launch traced here: 95.7 us
  Pallas kernels  88 us (92%)
  local copies, waits for them, and re-layouts  6.42 us (7%)
    pallas_call x1, Pallas kernels, on_device(): pl.pallas_call(kernel, out_shape=(jax.ShapeDtypeStruct((USERS, W), BF), j...  88 us
    unnamed x2, local copies, waits for them, and re-layouts  3.75 us

profile of v1, /device:TPU:0, one launch (start us, length us, event | category | flops | bytes accessed | tf_op | source)
XLA Modules:
  0.0 95.7 jit_solution(8733337709910229280)
XLA Ops:
  0.6 0.7 broadcast_subtract_fusion
  1.3 0.6 reshape.19.neg_lane
  1.9 0.7 reshape.20.neg_col
  2.6 1.4 %copy.7.pos_col = s32[128,1]{1,0:T(8,128)} copy(s32[128,1]{0,1:T(1,128)} %bitcast.2) | data formatting | bytes 1024 | tf_op jit(solution)/shard_map/reshape | solution.py:444
  4.0 88.0 %shard_map.68 = (bf16[128,2048]{1,0:T(8,128)(2,1)}, f32[64,2048]{1,0:T(8,128)}) custom-call(bf16[128,2048]{1,0:T(8,128)(2,1)} %user_hbm.1, bf16[2048,2048]{1,0:T(8,128)(2,1)} %proj_hbm.1, bf16[64,2048]{1,0:T(8,128)(2,1)} %tab.1, s32[1,128]{1,0:T(1,128)} %bitcast.3, s32[128,1]{1,0:T(8,128)} %copy.7.pos_col, s32[32,1]{1,0:T(8,128)} %reshape.20.neg_col, ...), custom_call_target="tpu_custom_call" | custom-call | flops 5000000000 | bytes 12582912 | tf_op jit(solution)/shard_map/pallas_call | solution.py:420
  92.0 1.9 %copy.11 = bf16[128,2048]{1,0:T(8,128)(2,1)} copy(bf16[128,2048]{1,0:T(8,128)(2,1)} %get-tuple-element.4) | data formatting | bytes 1048576
  93.8 1.9 %copy.12 = f32[64,2048]{1,0:T(8,128)} copy(f32[64,2048]{1,0:T(8,128)} %get-tuple-element.5) | data formatting | bytes 1048576

commit v2 on v1

--- a/solution.py
+++ b/solution.py
@@ -14,6 +14,7 @@
 HALF = W // 2
 CH = 512
 NC = W // CH
+EARLY = 4
 ROWS = 64
 USERS = 128
 SLOTS = 16
@@ -31,11 +32,11 @@
 
 
 def kernel(
-    user_hbm, proj_hbm, tab, pos_lane, pos_col, neg_col, neg_lane, ug_ref, ig_ref,
-    users, proj, hidden, z_ref, gh, probs, logits, pos_rows,
+    user_hbm, proj_hbm, tab_hbm, pos_hbm, neg_hbm, ug_ref, ig_ref,
+    tab, neg_ids, users, proj, hidden, z_ref, gh, probs, logits, pos_rows,
     shards, table, ids, pick_ref, slot_of, slot_to, send_slots, recv_slots, send_grads, recv_grads,
-    back, back_in, xs, xr, part, sib_in, r_left, r_right, r_a, r_b,
-    load_sem, ids_sem, shard_sem, slot_sem, grad_sem, back_sem, x_sem,
+    take_ref, weight_out, weights, back, back_in, xs, xr, part, sib_in, r_left, r_right, r_a, r_b,
+    load_sem, ids_sem, weight_sem, shard_sem, slot_sem, grad_sem, back_sem, x_sem,
     ag_send, ag_recv, sib_send, sib_recv, rs_send, rs_recv,
 ):
     scale = 4.0 / math.sqrt(W)
@@ -47,8 +48,9 @@
         return (gx, (lax.rem(zz + dz + 4, 4) * 4 + lax.rem(y + dy + 4, 4)) * 2 + cc)
 
     def mate(i):
-        u = lax.rem(me + i, 32)
-        return u, (u // 8, (lax.rem(u // 2, 4) * 4 + y) * 2 + lax.rem(u, 2))
+        p = i // 2
+        ux, uz, uc = lax.rem(g + p // 4 + p, 4), lax.rem(zz + p, 4), lax.rem(c + i, 2)
+        return (ux * 4 + uz) * 2 + uc, (ux, (uz * 4 + y) * 2 + uc)
 
     def xpeer(i):
         gx = lax.rem(g + i, 4)
@@ -77,6 +79,13 @@
     for dy in (1, 2, 3):
         pl.semaphore_signal(barrier, inc=1, device_id=dev(g, 0, dy, c), device_id_type=MESH)
 
+    first_loads = [
+        pltpu.make_async_copy(tab_hbm, tab, load_sem.at[5]),
+        pltpu.make_async_copy(neg_hbm, neg_ids, load_sem.at[6]),
+        pltpu.make_async_copy(pos_hbm, ids.at[me], load_sem.at[7]),
+    ]
+    for cp in first_loads:
+        cp.start()
     loads = [pltpu.make_async_copy(user_hbm, users, load_sem.at[0])]
     for t in range(NC):
         cols = pl.ds(t * CH, CH)
@@ -84,14 +93,23 @@
     for cp in loads:
         cp.start()
 
-    pick = (neg_col[...] == lax.broadcasted_iota(I32, (32, ROWS), 1)).astype(BF)
+    for cp in first_loads:
+        cp.wait()
+    pos_lane = ids.at[me]
+
+    diagonal = lax.broadcasted_iota(I32, (8, 8), 0) == lax.broadcasted_iota(I32, (8, 8), 1)
+    columns = []
+    for gi in range(4):
+        wide_ids = jnp.broadcast_to(neg_ids[gi:gi + 1, :], (8, 8)).astype(F32)
+        columns.append(jnp.sum(jnp.where(diagonal, wide_ids, 0.0), axis=1, keepdims=True))
+    neg_col = jnp.concatenate(columns, axis=0).astype(I32) - (g * 32 + m) * ROWS
+    pick = (neg_col == lax.broadcasted_iota(I32, (32, ROWS), 1)).astype(BF)
     picked = dot(pick, tab[...])
     for gi in range(4):
         rows8 = picked[8 * gi:8 * gi + 8, :]
         xs[gi] = jnp.concatenate([rows8[:, :HALF], rows8[:, HALF:]], axis=0).astype(BF)
     my_shard = pl.ds(pl.multiple_of(y * ROWS, ROWS), ROWS)
     shards[my_shard, :] = tab[...]
-    ids[me] = pos_lane[...]
     pl.semaphore_wait(barrier, 34)
 
     for i in (1, 2, 3):
@@ -161,7 +179,8 @@
 
     lane = lax.broadcasted_iota(I32, (USERS, USERS), 1)
     sub = lax.broadcasted_iota(I32, (USERS, USERS), 0)
-    own_c, own_l = pos_col[...] >> 6, pos_lane[...] >> 6
+    own_l = pos_lane[...] >> 6
+    own_c = jnp.sum(jnp.where(lane == sub, own_l.astype(F32), 0.0), axis=1, keepdims=True).astype(I32)
     same = own_c == own_l
     rank_c = jnp.sum((same & (lane < sub)).astype(F32), axis=1, keepdims=True).astype(I32)
     rank_l = jnp.sum((same & (sub < lane)).astype(F32), axis=0, keepdims=True).astype(I32)
@@ -180,6 +199,7 @@
     hit = (wide >> 6) == owner_q
     before = dot(hit.astype(BF), (sub < lane).astype(BF))
     take = hit & (before == (s_iota & 3).astype(F32))
+    take_ref[...] = take.astype(F32)
     found = jnp.sum(jnp.where(take, (wide & 63) + 1, 0).astype(F32), axis=1, keepdims=True).astype(I32)
     q_col = (lax.broadcasted_iota(I32, (512, 1), 0) & (SLOTS - 1)) >> 2
     target = jnp.where(found > 0, q_col * ROWS + found - 1, -1)
@@ -208,6 +228,21 @@
         hidden[:, cols] = h
         z_ref[:, cols] = (h * jax.nn.sigmoid(h)).astype(BF)
 
+    def send_z(t):
+        cols = pl.ds(t * CH, CH)
+        send_grads[:, cols] = dot(slot_to[...], z_ref[:, cols]).astype(BF)
+
+        def out(i, carry):
+            u, to = mate(i)
+            remote(send_grads.at[my_slots(u), cols], recv_grads.at[my_slots(me), cols], grad_sem.at[0, t], grad_sem.at[1, t], to)
+            return carry
+
+        lax.fori_loop(1, 32, out, 0)
+        recv_grads[my_slots(me), cols] = send_grads[my_slots(me), cols]
+
+    loads[0].wait()
+    for t in range(NC):
+        project(t)
     here(-1, 0, FULL, 0)
     push(-1, 0, LEFT, True, 1, 0)
     here(1, 0, FULL, 0)
@@ -221,16 +256,13 @@
     second(2, LEFT, 0)
     here(2, 0, RIGHT, 1)
     second(2, RIGHT, 1)
-    loads[0].wait()
-    project(0)
     gather(2)
     relay(-1, [(FULL, 0)])
-    project(1)
+    gather(3)
     relay(1, [(FULL, 0)])
-    gather(3)
-    project(2)
     relay(2, [(LEFT, 0), (RIGHT, 1)])
-    project(3)
+    for t in range(EARLY):
+        send_z(t)
     for f in RING:
         here(f, 2, LEFT, 0)
         over(f, 2, LEFT, 0)
@@ -261,18 +293,16 @@
     probs[...] = jnp.exp(lg - log_total).astype(BF)
     pos_weight = jnp.exp(pos_logit - log_total) - 1.0
 
-    for t in range(NC):
-        cols = pl.ds(t * CH, CH)
-        term = ((scale * pos_weight) * z_ref[:, cols].astype(F32)).astype(BF)
-        send_grads[:, cols] = dot(slot_to[...], term).astype(BF)
-
-        def out(i, carry, cols=cols, t=t):
-            u, to = mate(i)
-            remote(send_grads.at[my_slots(u), cols], recv_grads.at[my_slots(me), cols], grad_sem.at[0, t], grad_sem.at[1, t], to)
-            return carry
-
-        lax.fori_loop(1, 32, out, 0)
-        recv_grads[my_slots(me), cols] = send_grads[my_slots(me), cols]
+    weight_out[...] = jnp.sum(jnp.where(lane == sub, pos_weight, 0.0), axis=0, keepdims=True)
+    weights[me] = weight_out[...]
+
+    def send_weights(i, carry):
+        remote(weight_out, weights.at[me], weight_sem.at[0], weight_sem.at[1], mate(i)[1])
+        return carry
+
+    lax.fori_loop(1, 32, send_weights, 0)
+    for t in range(EARLY, NC):
+        send_z(t)
 
     def line(cc, dz):
         return pl.ds(pl.multiple_of((cc * 4 + lax.rem(zz + dz + 4, 4)) * 128, 128), 128)
@@ -338,7 +368,7 @@
     def gather_back(t):
         cols = pl.ds(t * CH, CH)
         arrive(recv_grads.at[pl.ds(0, 31 * SLOTS), cols], grad_sem.at[1, t])
-        back[:, cols] = dot(pick_ref[...], recv_grads[:, cols], 0, 0).astype(BF)
+        back[:, cols] = (scale * dot(pick_ref[...], recv_grads[:, cols], 0, 0)).astype(BF)
         for dy in (1, 3, 2):
             src = pl.ds(pl.multiple_of(lax.rem(y + dy, 4) * ROWS, ROWS), ROWS)
             remote(back.at[src, cols], back_in.at[my_shard, cols], back_sem.at[0, t], back_sem.at[1, t], dev(g, 0, dy, c))
@@ -352,6 +382,10 @@
     rings[2][1]()
     slope(3)
     rings[3][1]()
+    arrive(weights.at[pl.ds(0, 31)], weight_sem.at[1])
+    wide_w = jnp.broadcast_to(weights[...], (32, SLOTS, USERS)).reshape(512, USERS)
+    slot_w = jnp.sum(take_ref[...] * wide_w, axis=1, keepdims=True)
+    pick_ref[...] = (pick_ref[...].astype(F32) * slot_w).astype(BF)
     gather_back(0)
     lineup = ring(4, lambda d: block(c, d, 0), lambda s: dev(g, s, 0, c))
 
@@ -386,20 +420,18 @@
         v = xr[4 + gi].astype(F32)
         lines.append(jnp.concatenate([v[:8], v[8:]], axis=1))
     returned = jnp.concatenate(lines, axis=0).astype(BF)
-    place = (neg_lane[...] == lax.broadcasted_iota(I32, (ROWS, 32), 0)).astype(BF)
     for t in range(NC):
         cols = pl.ds(t * CH, CH)
         arrive(back_in.at[pl.ds(0, 192), cols], back_sem.at[1, t])
-        acc = dot(place, returned[:, t * CH:(t + 1) * CH])
+        acc = dot(pick, returned[:, t * CH:(t + 1) * CH], 0, 0)
         for q in range(4):
             acc = acc + back_in[pl.ds(q * ROWS, ROWS), cols].astype(F32)
         ig_ref[:, cols] = acc
 
-    for cp in late[:3]:
-        pass
     arrive(xs.at[pl.ds(0, 3)], x_sem.at[0])
     arrive(xs.at[pl.ds(4, 3)], x_sem.at[2])
     arrive(ids.at[pl.ds(0, 31)], ids_sem.at[0])
+    arrive(weights.at[pl.ds(0, 31)], weight_sem.at[0])
     for t in range(NC):
         cols = pl.ds(t * CH, CH)
         arrive(shards.at[pl.ds(0, 192), cols], shard_sem.at[0, t])
@@ -410,41 +442,49 @@
         cp.wait_send()
 
 
+def store(ug, ig, ug_out, ig_out, sem):
+    copies = [pltpu.make_async_copy(ug, ug_out, sem.at[0]), pltpu.make_async_copy(ig, ig_out, sem.at[1])]
+    for cp in copies:
+        cp.start()
+    for cp in copies:
+        cp.wait()
+
+
 def on_device(user_rows, projection, item_table, positive, negatives):
-    first_row = lax.axis_index(("grp", "mem")) * ROWS
-    local = negatives - first_row
     vm = pl.BlockSpec(memory_space=pltpu.VMEM)
     hbm = pl.BlockSpec(memory_space=pl.ANY)
     dma = pltpu.SemaphoreType.DMA
     v = pltpu.VMEM
-    return pl.pallas_call(
+    shapes = (jax.ShapeDtypeStruct((USERS, W), BF), jax.ShapeDtypeStruct((ROWS, W), F32))
+    user_grad, item_grad = pl.pallas_call(
         kernel,
-        out_shape=(jax.ShapeDtypeStruct((USERS, W), BF), jax.ShapeDtypeStruct((ROWS, W), F32)),
-        in_specs=[hbm, hbm, vm, vm, vm, vm, vm],
+        out_shape=shapes,
+        in_specs=[hbm] * 5,
         out_specs=(vm, vm),
         scratch_shapes=[
+            v((ROWS, W), BF), v((4, 8), I32),
             v((USERS, W), BF), v((W, W), BF), v((USERS, W), F32), v((USERS, W), BF), v((USERS, W), BF),
             v((USERS, 1024), BF), v((USERS, 1024), F32), v((USERS, W), F32),
             v((256, W), BF), v((1024, W), BF), v((32, 1, USERS), I32), v((512, 256), BF),
             v((USERS, 512), BF), v((512, USERS), BF),
             v((512, W), BF), v((512, W), BF), v((512, W), BF), v((512, W), BF),
+            v((512, USERS), F32), v((1, USERS), F32), v((32, 1, USERS), F32),
             v((256, W), BF), v((256, W), BF), v((8, 16, HALF), BF), v((8, 16, HALF), BF),
             v((1024, W), BF), v((4, 128, W), BF),
             v((5, 32, HALF), BF), v((5, 32, HALF), BF), v((5, 32, W), BF), v((5, 32, W), BF),
-            dma((5,)), dma((2,)), dma((2, NC)), dma((2, NC)), dma((2, NC)), dma((2, NC)), dma((4,)),
+            dma((8,)), dma((2,)), dma((2,)), dma((2, NC)), dma((2, NC)), dma((2, NC)), dma((2, NC)), dma((4,)),
             dma((40,)), dma((32,)), dma((32,)), dma((32,)), dma((24,)), dma((24,)),
         ],
-        compiler_params=pltpu.CompilerParams(collective_id=0, has_side_effects=True, vmem_limit_bytes=58 << 20),
+        compiler_params=pltpu.CompilerParams(collective_id=0, has_side_effects=True, vmem_limit_bytes=56 << 20),
         cost_estimate=pl.CostEstimate(flops=5 * 10**9, bytes_accessed=12 * 2**20, transcendentals=10**6),
-    )(
-        user_rows,
-        projection,
-        item_table,
-        positive.reshape(1, USERS),
-        positive.reshape(USERS, 1),
-        local.reshape(32, 1),
-        local.reshape(1, 32),
-    )
+    )(user_rows, projection, item_table, positive.reshape(1, USERS), negatives)
+    return pl.pallas_call(
+        store,
+        out_shape=shapes,
+        in_specs=[vm, vm],
+        out_specs=(hbm, hbm),
+        scratch_shapes=[dma((2,))],
+    )(user_grad, item_grad)
 
 
 def solution(mesh):

time: 96 us -> 89.5 us (0.932)
  local copies, waits for them, and re-layouts: 6.42 us -> 0 us
    unnamed x2 -> x0, local copies, waits for them, and re-layouts: 3.75 us -> none
    reshape x3 -> x0, local copies, waits for them, and re-layouts: 2.67 us -> none  [the longest x1 1.39 us: on_device(): positive.reshape(USERS, 1)]
    pallas_call x1 -> x2, Pallas kernels: 88 us -> 88.5 us  [the longest x1 86.3 us: on_device(): pl.pallas_call(kernel, out_shape=shapes, in_specs=[hbm] * 5, out_specs=(v...]
where the time goes in v2:
time: 89.5 us; the launch traced here: 89.3 us
  Pallas kernels  88.5 us (99%)
    pallas_call x1, Pallas kernels, on_device(): pl.pallas_call(kernel, out_shape=shapes, in_specs=[hbm] * 5, out_specs=(v...  86.3 us
    pallas_call x1, Pallas kernels, on_device(): pl.pallas_call(store, out_shape=shapes, in_specs=[vm, vm], out_specs=(hbm...  2.18 us

profile of v2, /device:TPU:0, one launch (start us, length us, event | category | flops | bytes accessed | tf_op | source)
XLA Modules:
  0.0 89.3 jit_solution(4604568690370051969)
XLA Ops:
  0.6 86.3 %shard_map.68 = (bf16[128,2048]{1,0:T(8,128)(2,1)}, f32[64,2048]{1,0:T(8,128)}) custom-call(bf16[128,2048]{1,0:T(8,128)(2,1)} %user_hbm.1, bf16[2048,2048]{1,0:T(8,128)(2,1)} %proj_hbm.1, bf16[64,2048]{1,0:T(8,128)(2,1)} %tab_hbm.1, s32[1,128]{1,0:T(1,128)} %bitcast.1, s32[4,8]{1,0:T(4,128)} %neg_hbm.1), custom_call_target="tpu_custom_call" | custom-call | flops 5000000000 | bytes 12582912 | tf_op jit(solution)/shard_map/pallas_call | solution.py:459
  87.0 2.2 %shard_map.69 = (bf16[128,2048]{1,0:T(8,128)(2,1)}, f32[64,2048]{1,0:T(8,128)}) custom-call(bf16[128,2048]{1,0:T(8,128)(2,1)} %get-tuple-element.4.ug, f32[64,2048]{1,0:T(8,128)} %get-tuple-element.5.ig), custom_call_target="tpu_custom_call" | custom-call | tf_op jit(solution)/shard_map/pallas_call | solution.py:481

commit v3 on v2

--- a/solution.py
+++ b/solution.py
@@ -109,7 +109,8 @@
         rows8 = picked[8 * gi:8 * gi + 8, :]
         xs[gi] = jnp.concatenate([rows8[:, :HALF], rows8[:, HALF:]], axis=0).astype(BF)
     my_shard = pl.ds(pl.multiple_of(y * ROWS, ROWS), ROWS)
-    shards[my_shard, :] = tab[...]
+    for t in range(NC):
+        shards[t, my_shard, :] = tab[:, t * CH:(t + 1) * CH]
     pl.semaphore_wait(barrier, 34)
 
     for i in (1, 2, 3):
@@ -122,10 +123,12 @@
         return carry
 
     lax.fori_loop(1, 32, send_ids, 0)
-    for t in range(NC):
+    def send_shards(t):
+        cols = pl.ds(t * CH, CH)
         for dy in (1, 3, 2):
-            cols = pl.ds(t * CH, CH)
-            remote(tab.at[:, cols], shards.at[my_shard, cols], shard_sem.at[0, t], shard_sem.at[1, t], dev(g, 0, dy, c))
+            remote(tab.at[:, cols], shards.at[t, my_shard], shard_sem.at[0, t], shard_sem.at[1, t], dev(g, 0, dy, c))
+
+    send_shards(0)
 
     def block(cc, dz, dy):
         at = ((cc * 4 + lax.rem(zz + dz + 4, 4)) * 4 + lax.rem(y + dy + 4, 4)) * 32
@@ -176,6 +179,7 @@
     push(0, 0, FULL, True, 1, 0)
     push(0, 0, FULL, True, -1, 0)
     second(0, FULL, 0)
+    send_shards(1)
 
     lane = lax.broadcasted_iota(I32, (USERS, USERS), 1)
     sub = lax.broadcasted_iota(I32, (USERS, USERS), 0)
@@ -210,16 +214,16 @@
 
     def gather(t):
         cols = pl.ds(t * CH, CH)
-        arrive(shards.at[pl.ds(0, 192), cols], shard_sem.at[1, t])
-        send_slots[:, cols] = dot(pick_ref[...], shards[:, cols]).astype(BF)
+        arrive(shards.at[t, pl.ds(0, 192)], shard_sem.at[1, t])
+        send_slots[t] = dot(pick_ref[...], shards[t]).astype(BF)
 
         def out(i, carry):
             u, to = mate(i)
-            remote(send_slots.at[my_slots(u), cols], recv_slots.at[my_slots(me), cols], slot_sem.at[0, t], slot_sem.at[1, t], to)
+            remote(send_slots.at[t, my_slots(u)], recv_slots.at[t, my_slots(me)], slot_sem.at[0, t], slot_sem.at[1, t], to)
             return carry
 
         lax.fori_loop(1, 32, out, 0)
-        recv_slots[my_slots(me), cols] = send_slots[my_slots(me), cols]
+        recv_slots[t, my_slots(me)] = send_slots[t, my_slots(me)]
 
     def project(t):
         cols = pl.ds(t * CH, CH)
@@ -230,15 +234,15 @@
 
     def send_z(t):
         cols = pl.ds(t * CH, CH)
-        send_grads[:, cols] = dot(slot_to[...], z_ref[:, cols]).astype(BF)
+        send_grads[t] = dot(slot_to[...], z_ref[:, cols]).astype(BF)
 
         def out(i, carry):
             u, to = mate(i)
-            remote(send_grads.at[my_slots(u), cols], recv_grads.at[my_slots(me), cols], grad_sem.at[0, t], grad_sem.at[1, t], to)
+            remote(send_grads.at[t, my_slots(u)], recv_grads.at[t, my_slots(me)], grad_sem.at[0, t], grad_sem.at[1, t], to)
             return carry
 
         lax.fori_loop(1, 32, out, 0)
-        recv_grads[my_slots(me), cols] = send_grads[my_slots(me), cols]
+        recv_grads[t, my_slots(me)] = send_grads[t, my_slots(me)]
 
     loads[0].wait()
     for t in range(NC):
@@ -249,6 +253,8 @@
     push(1, 0, RIGHT, True, -1, 1)
     second(-1, FULL, 0)
     second(1, FULL, 0)
+    send_shards(2)
+    send_shards(3)
     gather(0)
     relay(0, [(FULL, 0)])
     gather(1)
@@ -256,11 +262,11 @@
     second(2, LEFT, 0)
     here(2, 0, RIGHT, 1)
     second(2, RIGHT, 1)
+    relay(-1, [(FULL, 0)])
     gather(2)
-    relay(-1, [(FULL, 0)])
-    gather(3)
     relay(1, [(FULL, 0)])
     relay(2, [(LEFT, 0), (RIGHT, 1)])
+    gather(3)
     for t in range(EARLY):
         send_z(t)
     for f in RING:
@@ -281,8 +287,8 @@
     pos_logit = jnp.zeros((USERS, 1), F32)
     for t in range(NC):
         cols = pl.ds(t * CH, CH)
-        arrive(recv_slots.at[pl.ds(0, 31 * SLOTS), cols], slot_sem.at[1, t])
-        pr = dot(slot_of[...], recv_slots[:, cols])
+        arrive(recv_slots.at[t, pl.ds(0, 31 * SLOTS)], slot_sem.at[1, t])
+        pr = dot(slot_of[...], recv_slots[t])
         pos_rows[:, cols] = pr
         pos_logit = pos_logit + jnp.sum(z_ref[:, cols].astype(F32) * pr, axis=1, keepdims=True)
     pos_logit = scale * pos_logit
@@ -314,7 +320,7 @@
             pt = probs[:, rows]
             for t in range(NC):
                 cols = pl.ds(t * CH, CH)
-                part[rows, cols] = (scale * dot(pt, z_ref[:, cols], 0, 0)).astype(BF)
+                part[rows, cols] = dot(pt, z_ref[:, cols], 0, 0).astype(BF)
         late.append(remote(part.at[line(1 - c, dz)], sib_in.at[i], rs_send.at[i], rs_recv.at[i], sib))
 
     rs_count = [4]
@@ -367,21 +373,21 @@
 
     def gather_back(t):
         cols = pl.ds(t * CH, CH)
-        arrive(recv_grads.at[pl.ds(0, 31 * SLOTS), cols], grad_sem.at[1, t])
-        back[:, cols] = (scale * dot(pick_ref[...], recv_grads[:, cols], 0, 0)).astype(BF)
+        arrive(recv_grads.at[t, pl.ds(0, 31 * SLOTS)], grad_sem.at[1, t])
+        back[t] = dot(pick_ref[...], recv_grads[t], 0, 0).astype(BF)
         for dy in (1, 3, 2):
             src = pl.ds(pl.multiple_of(lax.rem(y + dy, 4) * ROWS, ROWS), ROWS)
-            remote(back.at[src, cols], back_in.at[my_shard, cols], back_sem.at[0, t], back_sem.at[1, t], dev(g, 0, dy, c))
-        back_in[my_shard, cols] = back[my_shard, cols]
+            remote(back.at[t, src], back_in.at[t, my_shard], back_sem.at[0, t], back_sem.at[1, t], dev(g, 0, dy, c))
+        back_in[t, my_shard] = back[t, my_shard]
 
     slope(0)
     rings[0][1]()
+    rings[1][1]()
     slope(1)
-    rings[1][1]()
+    rings[2][1]()
+    rings[3][1]()
     slope(2)
-    rings[2][1]()
     slope(3)
-    rings[3][1]()
     arrive(weights.at[pl.ds(0, 31)], weight_sem.at[1])
     wide_w = jnp.broadcast_to(weights[...], (32, SLOTS, USERS)).reshape(512, USERS)
     slot_w = jnp.sum(take_ref[...] * wide_w, axis=1, keepdims=True)
@@ -422,11 +428,11 @@
     returned = jnp.concatenate(lines, axis=0).astype(BF)
     for t in range(NC):
         cols = pl.ds(t * CH, CH)
-        arrive(back_in.at[pl.ds(0, 192), cols], back_sem.at[1, t])
+        arrive(back_in.at[t, pl.ds(0, 192)], back_sem.at[1, t])
         acc = dot(pick, returned[:, t * CH:(t + 1) * CH], 0, 0)
         for q in range(4):
-            acc = acc + back_in[pl.ds(q * ROWS, ROWS), cols].astype(F32)
-        ig_ref[:, cols] = acc
+            acc = acc + back_in[t, pl.ds(q * ROWS, ROWS)].astype(F32)
+        ig_ref[:, cols] = scale * acc
 
     arrive(xs.at[pl.ds(0, 3)], x_sem.at[0])
     arrive(xs.at[pl.ds(4, 3)], x_sem.at[2])
@@ -434,16 +440,21 @@
     arrive(weights.at[pl.ds(0, 31)], weight_sem.at[0])
     for t in range(NC):
         cols = pl.ds(t * CH, CH)
-        arrive(shards.at[pl.ds(0, 192), cols], shard_sem.at[0, t])
-        arrive(send_slots.at[pl.ds(0, 31 * SLOTS), cols], slot_sem.at[0, t])
-        arrive(send_grads.at[pl.ds(0, 31 * SLOTS), cols], grad_sem.at[0, t])
-        arrive(back.at[pl.ds(0, 192), cols], back_sem.at[0, t])
+        arrive(shards.at[t, pl.ds(0, 192)], shard_sem.at[0, t])
+        arrive(send_slots.at[t, pl.ds(0, 31 * SLOTS)], slot_sem.at[0, t])
+        arrive(send_grads.at[t, pl.ds(0, 31 * SLOTS)], grad_sem.at[0, t])
+        arrive(back.at[t, pl.ds(0, 192)], back_sem.at[0, t])
     for cp in late[3:-3]:
         cp.wait_send()
 
 
 def store(ug, ig, ug_out, ig_out, sem):
-    copies = [pltpu.make_async_copy(ug, ug_out, sem.at[0]), pltpu.make_async_copy(ig, ig_out, sem.at[1])]
+    copies = []
+    for src, dst in ((ug, ug_out), (ig, ig_out)):
+        n = src.shape[0] // 4
+        for k in range(4):
+            rows = pl.ds(k * n, n)
+            copies.append(pltpu.make_async_copy(src.at[rows], dst.at[rows], sem.at[len(copies)]))
     for cp in copies:
         cp.start()
     for cp in copies:
@@ -465,11 +476,11 @@
             v((ROWS, W), BF), v((4, 8), I32),
             v((USERS, W), BF), v((W, W), BF), v((USERS, W), F32), v((USERS, W), BF), v((USERS, W), BF),
             v((USERS, 1024), BF), v((USERS, 1024), F32), v((USERS, W), F32),
-            v((256, W), BF), v((1024, W), BF), v((32, 1, USERS), I32), v((512, 256), BF),
+            v((NC, 256, CH), BF), v((1024, W), BF), v((32, 1, USERS), I32), v((512, 256), BF),
             v((USERS, 512), BF), v((512, USERS), BF),
-            v((512, W), BF), v((512, W), BF), v((512, W), BF), v((512, W), BF),
+            v((NC, 512, CH), BF), v((NC, 512, CH), BF), v((NC, 512, CH), BF), v((NC, 512, CH), BF),
             v((512, USERS), F32), v((1, USERS), F32), v((32, 1, USERS), F32),
-            v((256, W), BF), v((256, W), BF), v((8, 16, HALF), BF), v((8, 16, HALF), BF),
+            v((NC, 256, CH), BF), v((NC, 256, CH), BF), v((8, 16, HALF), BF), v((8, 16, HALF), BF),
             v((1024, W), BF), v((4, 128, W), BF),
             v((5, 32, HALF), BF), v((5, 32, HALF), BF), v((5, 32, W), BF), v((5, 32, W), BF),
             dma((8,)), dma((2,)), dma((2,)), dma((2, NC)), dma((2, NC)), dma((2, NC)), dma((2, NC)), dma((4,)),
@@ -483,7 +494,7 @@
         out_shape=shapes,
         in_specs=[vm, vm],
         out_specs=(hbm, hbm),
-        scratch_shapes=[dma((2,))],
+        scratch_shapes=[dma((8,))],
     )(user_grad, item_grad)
 
 

time: 89.5 us -> 88.7 us (level)
  Pallas kernels: 88.5 us -> 87.3 us
    pallas_call x1, Pallas kernels: 86.3 us -> 85 us  [on_device(): pl.pallas_call(kernel, out_shape=shapes, in_specs=[hbm] * 5, out_specs=(v...]
where the time goes in v3:
time: 88.7 us; the launch traced here: 88.1 us
  Pallas kernels  87.3 us (98%)
    pallas_call x1, Pallas kernels, on_device(): pl.pallas_call(kernel, out_shape=shapes, in_specs=[hbm] * 5, out_specs=(v...  85 us
    pallas_call x1, Pallas kernels, on_device(): pl.pallas_call(store, out_shape=shapes, in_specs=[vm, vm], out_specs=(hbm...  2.22 us

profile of v3, /device:TPU:0, one launch (start us, length us, event | category | flops | bytes accessed | tf_op | source)
XLA Modules:
  0.0 88.1 jit_solution(701634115520904230)
XLA Ops:
  0.6 85.0 %shard_map.68 = (bf16[128,2048]{1,0:T(8,128)(2,1)}, f32[64,2048]{1,0:T(8,128)}) custom-call(bf16[128,2048]{1,0:T(8,128)(2,1)} %user_hbm.1, bf16[2048,2048]{1,0:T(8,128)(2,1)} %proj_hbm.1, bf16[64,2048]{1,0:T(8,128)(2,1)} %tab_hbm.1, s32[1,128]{1,0:T(1,128)} %bitcast.1, s32[4,8]{1,0:T(4,128)} %neg_hbm.1), custom_call_target="tpu_custom_call" | custom-call | flops 5000000000 | bytes 12582912 | tf_op jit(solution)/shard_map/pallas_call | solution.py:470
  85.7 2.2 %shard_map.69 = (bf16[128,2048]{1,0:T(8,128)(2,1)}, f32[64,2048]{1,0:T(8,128)}) custom-call(bf16[128,2048]{1,0:T(8,128)(2,1)} %get-tuple-element.4.ug, f32[64,2048]{1,0:T(8,128)} %get-tuple-element.5.ig), custom_call_target="tpu_custom_call" | custom-call | tf_op jit(solution)/shard_map/pallas_call | solution.py:492

commit v4 on v3

--- a/solution.py
+++ b/solution.py
@@ -253,11 +253,11 @@
     push(1, 0, RIGHT, True, -1, 1)
     second(-1, FULL, 0)
     second(1, FULL, 0)
+    gather(0)
     send_shards(2)
-    send_shards(3)
-    gather(0)
     relay(0, [(FULL, 0)])
     gather(1)
+    send_shards(3)
     here(2, 0, LEFT, 0)
     second(2, LEFT, 0)
     here(2, 0, RIGHT, 1)
@@ -392,7 +392,6 @@
     wide_w = jnp.broadcast_to(weights[...], (32, SLOTS, USERS)).reshape(512, USERS)
     slot_w = jnp.sum(take_ref[...] * wide_w, axis=1, keepdims=True)
     pick_ref[...] = (pick_ref[...].astype(F32) * slot_w).astype(BF)
-    gather_back(0)
     lineup = ring(4, lambda d: block(c, d, 0), lambda s: dev(g, s, 0, c))
 
     def settle(i):
@@ -400,6 +399,7 @@
 
     settle(0)
     lineup[0]()
+    gather_back(0)
     user(0)
     settle(1)
     settle(2)

time: 88.7 us -> 88.3 us (level)
  no operation moved by 1% of the time
where the time goes in v4:
time: 88.3 us; the launch traced here: 88.1 us
  Pallas kernels  87.3 us (99%)
    pallas_call x1, Pallas kernels, on_device(): pl.pallas_call(kernel, out_shape=shapes, in_specs=[hbm] * 5, out_specs=(v...  85.1 us
    pallas_call x1, Pallas kernels, on_device(): pl.pallas_call(store, out_shape=shapes, in_specs=[vm, vm], out_specs=(hbm...  2.22 us

profile of v4, /device:TPU:0, one launch (start us, length us, event | category | flops | bytes accessed | tf_op | source)
XLA Modules:
  0.0 88.1 jit_solution(14660784697228909396)
XLA Ops:
  0.6 85.1 %shard_map.68 = (bf16[128,2048]{1,0:T(8,128)(2,1)}, f32[64,2048]{1,0:T(8,128)}) custom-call(bf16[128,2048]{1,0:T(8,128)(2,1)} %user_hbm.1, bf16[2048,2048]{1,0:T(8,128)(2,1)} %proj_hbm.1, bf16[64,2048]{1,0:T(8,128)(2,1)} %tab_hbm.1, s32[1,128]{1,0:T(1,128)} %bitcast.1, s32[4,8]{1,0:T(4,128)} %neg_hbm.1), custom_call_target="tpu_custom_call" | custom-call | flops 5000000000 | bytes 12582912 | tf_op jit(solution)/shard_map/pallas_call | solution.py:470
  85.7 2.2 %shard_map.69 = (bf16[128,2048]{1,0:T(8,128)(2,1)}, f32[64,2048]{1,0:T(8,128)}) custom-call(bf16[128,2048]{1,0:T(8,128)(2,1)} %get-tuple-element.4.ug, f32[64,2048]{1,0:T(8,128)} %get-tuple-element.5.ig), custom_call_target="tpu_custom_call" | custom-call | tf_op jit(solution)/shard_map/pallas_call | solution.py:492
